TPU v7x, 32 devices: a whole 2x2x4 slice. The times are simulated.
32 devices in a mesh: seq: 16 (over z, y, x), doc: 2 (over core).
Axes of the slice: x: 2, y: 2, z: 4, core: 2. Of those that a mesh axis runs over, the one named last changes fastest.
Arguments:
- conv_input: bfloat16 [4096, 4352], P(('doc', 'seq')), parts along dimension 0, may hold values from -6 to 6
- gate_input: bfloat16 [4096, 4096], P(('doc', 'seq')), parts along dimension 0, may hold values from -6 to 6
- step_input: bfloat16 [4096, 64], P(('doc', 'seq')), parts along dimension 0, may hold values from -1.1 to 2.9
- conv_weight: float32 [4, 4352], replicated, may hold values from -3 to 3
- convolution_bias: float32 [4352], replicated, may hold values from -0.5 to 0.5
- step_bias: float32 [64], replicated, may hold values from -12 to -2, as said below
- decay_log: float32 [64], replicated, may hold values from -3.3 to -1, as said below
- skip_gain: float32 [64], replicated, may hold values from 0.5 to 2
- norm_gain: float32 [4096], replicated, may hold values from 0.5 to 1.5
Outputs:
- normed: bfloat16 [4096, 4096], P(('doc', 'seq')), parts along dimension 0
There are 2 independent parts, one for each index of `doc`. A program takes and returns all parts, laid end to end along the dimension named above; an argument that names none is the same for every part. Nothing has to cross between parts.
Inputs may be any that keep to these rules, and one draw needn't show every extreme that they name: `decay_log`: one value a head. `step_bias`: one value a head.
All inputs are finite; a program needn't handle non-finite values.
Results may differ from a plain program's by a relative error of at most 0.0051.
Values may be sent and summed in bfloat16 or wider, within the bound.
A program may use at most 64 MiB of HBM per device.

v0:
```python
import jax
import jax.numpy as jnp
from jax import lax
from jax.sharding import PartitionSpec as P

HEADDIM = 64
STATE = 128
HEADS = 64
STRETCH = 256


def shifted(value, axis, steps):
    count = lax.axis_size(axis)
    initial, last = (max(0, -steps), min(count, count - steps))
    return lax.ppermute(value, axis, [(source, source + steps) for source in range(initial, last)])


def gated_norm(mixed_out, gate_input, norm_gain):
    gated = mixed_out.astype(jnp.float32) * jax.nn.silu(gate_input.astype(jnp.float32))
    spread = jnp.mean(gated * gated, axis=-1, keepdims=True)
    return (gated * lax.rsqrt(spread + 1e-05) * norm_gain[None, :]).astype(jnp.bfloat16)


def convolve(conv_input, conv_weight, convolution_bias):
    tap_count = conv_weight.shape[0]
    row_count = conv_input.shape[0]
    earlier = shifted(conv_input[row_count - (tap_count - 1) :], "seq", 1)
    padded = jnp.concatenate([earlier, conv_input], axis=0).astype(jnp.float32)
    mixed = convolution_bias[None, :]
    for offset in range(tap_count):
        mixed = mixed + conv_weight[offset][None, :] * padded[offset : offset + row_count]
    return jax.nn.silu(mixed).astype(jnp.bfloat16)


def dual_form(values, step_size, decay_rate, b_rows, c_rows, block_len):
    highest = lax.Precision.HIGHEST
    row_count, head_count, head_width = values.shape
    state_width = b_rows.shape[1]
    blocks = row_count // block_len
    block_values = values.reshape(blocks, block_len, head_count, head_width)
    block_step_sizes = step_size.reshape(blocks, block_len, head_count)
    block_b = b_rows.reshape(blocks, block_len, state_width)
    block_c = c_rows.reshape(blocks, block_len, state_width)
    within = jnp.cumsum(block_step_sizes * decay_rate[None, None, :], axis=1)
    ends = within[:, -1, :]
    totals = jnp.cumsum(ends, axis=0)
    before = totals - ends
    lower = jnp.arange(block_len)[:, None] >= jnp.arange(block_len)[None, :]
    turned = jnp.transpose(within, (0, 2, 1))
    diffs = jnp.where(lower[None, None], turned[:, :, :, None] - turned[:, :, None, :], -jnp.inf)
    scores = jnp.einsum("ctn,csn->cts", block_c, block_b, precision=highest)
    mixing = (
        jnp.exp(diffs) * scores[:, None] * jnp.transpose(block_step_sizes, (0, 2, 1))[:, :, None, :]
    )
    inside = jnp.einsum("chts,cshp->cthp", mixing, block_values, precision=highest)
    tail = jnp.exp(ends[:, None, :] - within) * block_step_sizes
    weighted = tail[:, :, :, None] * block_values
    states = jnp.einsum("cshp,csn->chpn", weighted, block_b, precision=highest)
    order = jnp.arange(blocks)
    earlier_mask = order[:, None] > order[None, :]
    gap = jnp.where(earlier_mask[None], before.T[:, :, None] - totals.T[:, None, :], -jnp.inf)
    entering = jnp.einsum("hcd,dhpn->chpn", jnp.exp(gap), states, precision=highest)
    outside = jnp.exp(within)[:, :, :, None] * jnp.einsum(
        "ctn,chpn->cthp", block_c, entering, precision=highest
    )
    result = (inside + outside).reshape(row_count, head_count, head_width)
    last = totals[-1]
    final = jnp.einsum("dh,dhpn->hpn", jnp.exp(last[None, :] - totals), states, precision=highest)
    decay_sum = (before[:, None, :] + within).reshape(row_count, head_count)
    return (result, final, decay_sum, last)


def shards(
    conv_input,
    gate_input,
    step_input,
    conv_weight,
    convolution_bias,
    step_bias,
    decay_log,
    skip_gain,
    norm_gain,
):
    inner_width = HEADS * HEADDIM
    decay_rate = -jnp.exp(decay_log)
    activated = convolve(conv_input, conv_weight, convolution_bias)
    head_values, head_steps = (
        lax.all_to_all(activated[:, :inner_width], "seq", split_axis=1, concat_axis=0, tiled=True),
        lax.all_to_all(step_input, "seq", split_axis=1, concat_axis=0, tiled=True),
    )
    shared = lax.all_gather(activated[:, inner_width:], "seq", axis=0, tiled=True)
    full_rows = shared.shape[0]
    own_heads = head_steps.shape[1]
    first_head = lax.axis_index("seq") * own_heads
    own_bias = lax.dynamic_slice_in_dim(step_bias, first_head, own_heads)
    own_rate = lax.dynamic_slice_in_dim(decay_rate, first_head, own_heads)
    own_skip = lax.dynamic_slice_in_dim(skip_gain, first_head, own_heads)
    values = head_values.astype(jnp.float32).reshape(full_rows, own_heads, HEADDIM)
    shared_rows = shared.astype(jnp.float32)
    step_size = jax.nn.softplus(head_steps.astype(jnp.float32) + own_bias[None, :])
    result, final, decay_sum, last = dual_form(
        values,
        step_size,
        own_rate,
        shared_rows[:, :STATE],
        shared_rows[:, STATE:],
        min(STRETCH, full_rows),
    )
    result = result + own_skip[None, :, None] * values
    head_output = result.astype(jnp.bfloat16).reshape(full_rows, own_heads * HEADDIM)
    mixed_out = lax.all_to_all(head_output, "seq", split_axis=0, concat_axis=1, tiled=True)
    return gated_norm(mixed_out, gate_input, norm_gain)


def solution(mesh):
    in_specs = (
        P(("doc", "seq"), None),
        P(("doc", "seq"), None),
        P(("doc", "seq"), None),
        P(),
        P(),
        P(),
        P(),
        P(),
        P(),
    )
    out_specs = P(("doc", "seq"), None)
    return jax.shard_map(shards, mesh=mesh, in_specs=in_specs, out_specs=out_specs, check_vma=False)
```

profile of v0, /device:TPU:0, one launch (start us, length us, event | category | flops | bytes accessed | tf_op | source)
XLA Modules:
  0.0 146.6 jit_solution(9924083408817625690)
XLA Ops:
  6.5 8.4 %all-to-all-start.1 = ((bf16[128,16,4]{0,2,1:T(4,128)(2,1)}), bf16[128,16,4]{0,2,1:T(4,128)(2,1)S(1)}, u32[]{:S(2)}, u32[]{:S(2)}) async-start(bf16[128,16,4]{0,2,1:T(4,128)(2,1)} %bitcast.77), calls=%async_computation.1 | async-start | bytes 32768 | tf_op jit(solution)/shard_map/all_to_all | solution.py:89
  15.0 0.9 slice.49
  15.9 3.8 %collective-permute-start = (bf16[3,4352]{1,0:T(4,128)(2,1)S(1)}, bf16[3,4352]{1,0:T(4,128)(2,1)S(1)}, u32[]{:S(2)}, u32[]{:S(2)}) collective-permute-start(bf16[3,4352]{1,0:T(4,128)(2,1)S(1)} %slice.49), channel_id=1, source_target_pairs={{0,2},{2,4},{4,6},{6,8},{8,10},{10,12},{12,14},{14,16},{16,18},{18... | collective-permute-start | bytes 78344 | tf_op jit(solution)/shard_map/ppermute | solution.py:15
  19.8 1.2 slice_reduce_fusion.4
  21.0 1.7 %copy.46 = bf16[128,4352]{0,1:T(8,128)(2,1)S(1)} copy(bf16[128,4352]{1,0:T(8,128)(2,1)} %param.9) | data formatting | bytes 2228224 | tf_op args[0]
  24.2 5.5 %multiply_convert_fusion = bf16[128,4352]{0,1:T(8,128)(2,1)S(1)} fusion(f32[131,4352]{0,1:T(8,128)S(1)} %maximum_convert_fusion, f32[4352]{0:T(1024)S(1)} %get-tuple-element.7, f32[4352]{0:T(1024)S(1)} %get-tuple-element.8, f32[4352]{0:T(1024)S(1)} %get-tuple-element.6, f32[4352]{0:T(1024)S(1)} %get-tuple-element.5, f32[4352]{0:T(1024)S(1)} %copy-done.1), kind=kLoop, calls=%fused_computation.23 | loop fusion | flops 7241728 | bytes 10114048 | tf_op jit(solution)/shard_map/convert_element_type | solution.py:32
  29.7 1.0 slice.68
  31.4 5.9 %all-to-all-start = ((bf16[128,16,256]{0,2,1:T(8,128)(2,1)}), bf16[128,16,256]{0,2,1:T(8,128)(2,1)S(1)}, u32[]{:S(2)}, u32[]{:S(2)}) async-start(bf16[128,16,256]{0,2,1:T(8,128)(2,1)} %bitcast), calls=%async_computation | async-start | bytes 2097152 | tf_op jit(solution)/shard_map/all_to_all | solution.py:88
  37.8 2.3 %reduce-window.6 = f32[8,4,2,128]{3,0,1,2:T(8,128)S(1)} reduce-window(f32[8,4,2,128]{3,0,1,2:T(8,128)S(1)} %copy.49, f32[]{:T(128)} %constant.30.clone.1), window={size=1x1x1x128 pad=0_0x0_0x0_0x127_0}, to_apply=%region_0.1 | reduce-window | flops 1040384 | bytes 65540 | tf_op jit(solution)/shard_map/reduce-window
  40.9 21.0 %all-to-all-done = bf16[128,16,256]{0,2,1:T(8,128)(2,1)S(1)} async-done(((bf16[128,16,256]{0,2,1:T(8,128)(2,1)}), bf16[128,16,256]{0,2,1:T(8,128)(2,1)S(1)}, u32[]{:S(2)}, u32[]{:S(2)}) %all-to-all-start) | async-done | bytes 1048608 | tf_op jit(solution)/shard_map/all_to_all | solution.py:88
  63.2 24.1 %all-gather.2.cloned.1.call-done = bf16[2048,256]{0,1:T(8,128)(2,1)} async-done(((bf16[128,256]{0,1:T(8,128)(2,1)}), bf16[2048,256]{0,1:T(8,128)(2,1)}) %all-gather.2.cloned.1.call-update) | async-done | bytes 1048592 | tf_op jit(solution)/shard_map/all_gather | solution.py:91
  87.2 2.1 %fusion.41 = (bf16[2048,128]{0,1:T(8,128)(2,1)S(1)}, bf16[2048,128]{0,1:T(8,128)(2,1)}) fusion(bf16[2048,256]{0,1:T(8,128)(2,1)} %all-gather.2.cloned.1.call-done), kind=kLoop, calls=%fused_computation.71 | loop fusion | bytes 2097152 | tf_op jit(solution)/shard_map/slice | solution.py:105
  89.6 1.3 copy.53
  91.1 1.6 %fusion.21 = f32[8,4,64,128]{3,2,1,0:T(8,128)S(1)} fusion(bf16[8,256,128,1]{2,1,3,0:T(8,128)(2,1)S(1)} %bitcast.72, f32[8,256,4,64]{1,0,3,2:T(8,128)S(1)} %convert_multiply_fusion.1), kind=kOutput, calls=%fused_computation.31 | convolution fusion | flops 805306368 | bytes 3670016 | tf_op jit(solution)/shard_map/cshp,csn->chpn/dot_general | solution.py:58
  92.8 1.6 %convolution_bitcast_fusion = f32[8,4,64,128]{3,0,2,1:T(8,128)S(1)} fusion(f32[8,4,64,128]{3,2,1,0:T(8,128)S(1)} %fusion.21, f32[4,8]{1,0:T(4,128)S(1)} %bitcast.76, f32[4,8]{1,0:T(4,128)S(1)} %subtract_bitcast_fusion, pred[8,8]{1,0:T(8,128)(4,1)S(1)} %iota_compare_fusion.1), kind=kOutput, calls=%fused_computation.36 | convolution fusion | flops 25166336 | bytes 2097472 | tf_op jit(solution)/shard_map/hcd,dhpn->chpn/dot_general | solution.py:62
  94.4 1.0 fusion.25
  95.8 6.2 %bitcast_add_fusion = f32[8,256,4,64]{1,3,2,0:T(8,128)S(1)} fusion(f32[8,256,4,64]{1,3,2,0:T(8,128)S(1)} %fusion.25, f32[8,4,256]{2,1,0:T(4,128)S(1)} %copy.55, f32[8,256,256]{2,1,0:T(8,128)S(1)} %fusion.43, f32[8,4,256]{2,1,0:T(4,128)S(1)} %copy.51, pred[256,256]{1,0:T(8,128)(4,1)S(1)} %iota_compare_fusion, ...), kind=kOutput, calls=%fused_computation.28 | convolution fusion | flops 1620049920 | bytes 7503872 | tf_op jit(solution)/shard_map/chts,cshp->cthp/dot_general | solution.py:55
  102.0 2.8 %copy.61 = f32[8,256,4,64]{1,0,3,2:T(8,128)} copy(f32[8,256,4,64]{1,3,2,0:T(8,128)S(1)} %bitcast_add_fusion) | data formatting | bytes 4194304 | tf_op jit(solution)/shard_map/add | solution.py:66
  104.8 1.6 %reshape.121 = f32[16,128,256]{1,0,2:T(8,128)S(1)} reshape(f32[8,256,4,64]{1,0,3,2:T(8,128)} %copy.61) | data formatting | bytes 4194304 | tf_op jit(solution)/shard_map/reshape | solution.py:66
  106.4 1.7 %fusion.20 = bf16[16,128,256]{1,2,0:T(8,128)(2,1)} fusion(f32[16,128,256]{1,0,2:T(8,128)S(1)} %reshape.121, f32[256]{0:T(256)S(1)} %mul.156, bf16[128,16,256]{0,2,1:T(8,128)(2,1)S(1)} %all-to-all-done), kind=kLoop, calls=%fused_computation.30 | loop fusion | flops 2097152 | bytes 4195328 | tf_op jit(solution)/shard_map/convert_element_type | solution.py:110
  108.1 4.6 %all-to-all-start.2 = ((bf16[16,128,256]{1,2,0:T(8,128)(2,1)}), bf16[16,128,256]{1,2,0:T(8,128)(2,1)S(1)}, u32[]{:S(2)}, u32[]{:S(2)}) async-start(bf16[16,128,256]{1,2,0:T(8,128)(2,1)} %fusion.20), calls=%async_computation.2 | async-start | bytes 2097152 | tf_op jit(solution)/shard_map/all_to_all | solution.py:111
  113.4 23.4 %all-to-all-done.2 = bf16[16,128,256]{1,2,0:T(8,128)(2,1)S(1)} async-done(((bf16[16,128,256]{1,2,0:T(8,128)(2,1)}), bf16[16,128,256]{1,2,0:T(8,128)(2,1)S(1)}, u32[]{:S(2)}, u32[]{:S(2)}) %all-to-all-start.2) | async-done | bytes 1048608 | tf_op jit(solution)/shard_map/all_to_all | solution.py:111
  137.5 0.9 multiply_convert_fusion.1
  138.4 1.3 copy.64
  (51 shorter events, 6.9 us)
Async XLA Ops:
  6.5 16.2 %copy-start.3 = (f32[64]{0:T(128)S(1)}, f32[64]{0:T(128)}, u32[]{:S(2)}) copy-start(f32[64]{0:T(128)} %param.14) | copy-start | bytes 772
  6.5 24.9 %all-to-all-start.1 = ((bf16[128,16,4]{0,2,1:T(4,128)(2,1)}), bf16[128,16,4]{0,2,1:T(4,128)(2,1)S(1)}, u32[]{:S(2)}, u32[]{:S(2)}) async-start(bf16[128,16,4]{0,2,1:T(4,128)(2,1)} %bitcast.77), calls=%async_computation.1 | async-start | bytes 32768 | tf_op jit(solution)/shard_map/all_to_all | solution.py:89
  15.0 72.3 %all-gather.2.cloned.1.call-start = ((), (), s32[]{:S(2)}) async-start(), calls=%async_computation.3 | async-start | bytes 1114112 | tf_op jit(solution)/shard_map/all_gather | solution.py:91
  15.9 6.9 %collective-permute-start = (bf16[3,4352]{1,0:T(4,128)(2,1)S(1)}, bf16[3,4352]{1,0:T(4,128)(2,1)S(1)}, u32[]{:S(2)}, u32[]{:S(2)}) collective-permute-start(bf16[3,4352]{1,0:T(4,128)(2,1)S(1)} %slice.49), channel_id=1, source_target_pairs={{0,2},{2,4},{4,6},{6,8},{8,10},{10,12},{12,14},{14,16},{16,18},{18... | collective-permute-start | bytes 78344 | tf_op jit(solution)/shard_map/ppermute | solution.py:15
  23.3 0.8 copy-start.1
  29.7 7.6 %copy-start.4 = (f32[64]{0:T(128)S(1)}, f32[64]{0:T(128)}, u32[]{:S(2)}) copy-start(f32[64]{0:T(128)} %param.15) | copy-start | bytes 772
  29.7 7.7 %copy-start.5 = (f32[64]{0:T(128)S(1)}, f32[64]{0:T(128)}, u32[]{:S(2)}) copy-start(f32[64]{0:T(128)} %param.16) | copy-start | bytes 772
  31.4 30.5 %all-to-all-start = ((bf16[128,16,256]{0,2,1:T(8,128)(2,1)}), bf16[128,16,256]{0,2,1:T(8,128)(2,1)S(1)}, u32[]{:S(2)}, u32[]{:S(2)}) async-start(bf16[128,16,256]{0,2,1:T(8,128)(2,1)} %bitcast), calls=%async_computation | async-start | bytes 2097152 | tf_op jit(solution)/shard_map/all_to_all | solution.py:88
  108.1 4.6 %copy-start = (bf16[128,4096]{1,0:T(8,128)(2,1)S(1)}, bf16[128,4096]{1,0:T(8,128)(2,1)}, u32[]{:S(2)}) copy-start(bf16[128,4096]{1,0:T(8,128)(2,1)} %param.10) | copy-start | bytes 3145732
  108.1 28.7 %all-to-all-start.2 = ((bf16[16,128,256]{1,2,0:T(8,128)(2,1)}), bf16[16,128,256]{1,2,0:T(8,128)(2,1)S(1)}, u32[]{:S(2)}, u32[]{:S(2)}) async-start(bf16[16,128,256]{1,2,0:T(8,128)(2,1)} %fusion.20), calls=%async_computation.2 | async-start | bytes 2097152 | tf_op jit(solution)/shard_map/all_to_all | solution.py:111
  112.8 24.8 %copy-start.2 = (f32[4096]{0:T(1024)S(1)}, f32[4096]{0:T(1024)}, u32[]{:S(2)}) copy-start(f32[4096]{0:T(1024)} %param.17) | copy-start | bytes 49156
Sparse Core Ops, SparseCore 0:
  31.5 55.6 all-gather.1
where the time goes:
time: 147 us
  waiting for transfers between devices  68.4 us (47%)
  starting transfers between devices  22.8 us (16%)
  local copies, waits for them, and re-layouts  18.1 us (12%)
  between operations  13.7 us (9%)
  other arithmetic  12.6 us (9%)
  matrix products  10.8 us (7%)
    all_gather x1, waiting for transfers between devices, shards(): lax.all_gather(activated[:, inner_width:], 'seq', axis=0, tiled=True)  24.1 us
    all_to_all x1, waiting for transfers between devices, shards(): lax.all_to_all(head_output, 'seq', split_axis=0, concat_axis=1, tiled=True)  23.4 us
    all_to_all x1, waiting for transfers between devices, shards(): lax.all_to_all(activated[:, :inner_width], 'seq', split_axis=1, concat_ax...  21 us
    all_to_all x1, starting transfers between devices, shards(): lax.all_to_all(step_input, 'seq', split_axis=1, concat_axis=0, tiled=True)  8.44 us
    dot_general x1, matrix products, dual_form(): jnp.einsum('chts,cshp->cthp', mixing, block_values, precision=highest)  6.18 us
    all_to_all x1, starting transfers between devices, shards(): lax.all_to_all(activated[:, :inner_width], 'seq', split_axis=1, concat_ax...  5.89 us
    convert_element_type x1, other arithmetic, convolve(): return jax.nn.silu(mixed).astype(jnp.bfloat16)  5.49 us
    all_to_all x1, starting transfers between devices, shards(): lax.all_to_all(head_output, 'seq', split_axis=0, concat_axis=1, tiled=True)  4.62 us
  transfers between devices with their start and end apart: 5, of which 3 were waited for; matrix products, arithmetic and copies ran while one was open for 12% of the time, Pallas kernels for 0%

commit v1 on v0

--- a/solution.py
+++ b/solution.py
@@ -7,6 +7,29 @@
 STATE = 128
 HEADS = 64
 STRETCH = 256
+
+
+def split_up(shard, dim, count):
+    lengths = shard.shape
+    parts = shard.reshape(*lengths[:dim], count, lengths[dim] // count, *lengths[dim + 1 :])
+    return jnp.moveaxis(parts, dim, 0)
+
+
+def joined_along(parts, dim):
+    parts = jnp.moveaxis(parts, 0, dim)
+    shape = parts.shape
+    return parts.reshape(*shape[:dim], shape[dim] * shape[dim + 1], *shape[dim + 2 :])
+
+
+def exchange_in_pairs(array, axis, split_dim, concat_dim):
+    length, index = (lax.axis_size(axis), lax.axis_index(axis))
+    blocks = split_up(array, split_dim, length)
+    done = [blocks[index]]
+    for step in range(1, length):
+        sent = blocks[index ^ step]
+        done.append(lax.ppermute(sent, axis, [(i, i ^ step) for i in range(length)]))
+    blocks = jnp.stack(done)[index ^ jnp.arange(length)]
+    return joined_along(blocks, concat_dim)
 
 
 def shifted(value, axis, steps):
@@ -85,7 +108,7 @@
     decay_rate = -jnp.exp(decay_log)
     activated = convolve(conv_input, conv_weight, convolution_bias)
     head_values, head_steps = (
-        lax.all_to_all(activated[:, :inner_width], "seq", split_axis=1, concat_axis=0, tiled=True),
+        exchange_in_pairs(activated[:, :inner_width], "seq", 1, 0),
         lax.all_to_all(step_input, "seq", split_axis=1, concat_axis=0, tiled=True),
     )
     shared = lax.all_gather(activated[:, inner_width:], "seq", axis=0, tiled=True)

time: 147 us -> 167 us (1.14)
  starting transfers between devices: 22.8 us -> 46 us
  waiting for transfers between devices: 68.4 us -> 47.3 us
  local copies, waits for them, and re-layouts: 18.1 us -> 30.2 us
  other arithmetic: 12.6 us -> 16.5 us
    ppermute x0 -> x15, starting transfers between devices: none -> 30.5 us  [exchange_in_pairs(): lax.ppermute(sent, axis, [(i, i ^ step) for i in range(length)])]
    all_to_all x1 -> x0, waiting for transfers between devices: 21 us -> none  [shards(): lax.all_to_all(activated[:, :inner_width], 'seq', split_axis=1, concat_ax...]
    all_to_all x1 -> x0, starting transfers between devices: 5.89 us -> none  [shards(): lax.all_to_all(activated[:, :inner_width], 'seq', split_axis=1, concat_ax...]
    all_gather x1, waiting for transfers between devices: 24.1 us -> 18.2 us  [shards(): lax.all_gather(activated[:, inner_width:], 'seq', axis=0, tiled=True)]
    ppermute x0 -> x15, waiting for transfers between devices: none -> 5.74 us  [exchange_in_pairs(): lax.ppermute(sent, axis, [(i, i ^ step) for i in range(length)])]
    reshape x1 -> x2, local copies, waits for them, and re-layouts: 1.63 us -> 7.34 us  [dual_form(): result = (inside + outside).reshape(row_count, head_count, head_width)]
    add x1 -> x0, local copies, waits for them, and re-layouts: 2.79 us -> none  [dual_form(): result = (inside + outside).reshape(row_count, head_count, head_width)]
    all_to_all x1, starting transfers between devices: 8.44 us -> 5.95 us  [shards(): lax.all_to_all(step_input, 'seq', split_axis=1, concat_axis=0, tiled=True)]
  transfers between devices with their start and end apart: 5 -> 19, of which waited for: 3 -> 5; matrix products, arithmetic and copies ran while one was open for 12% -> 13% of each run, Pallas kernels for 0% -> 0%
where the time goes in v1:
time: 167 us; the launch traced here: 166 us
  waiting for transfers between devices  47.3 us (28%)
  starting transfers between devices  46 us (28%)
  local copies, waits for them, and re-layouts  30.2 us (18%)
  other arithmetic  16.5 us (10%)
  between operations  13.9 us (8%)
  matrix products  11.9 us (7%)
    ppermute x15, starting transfers between devices, exchange_in_pairs(): lax.ppermute(sent, axis, [(i, i ^ step) for i in range(length)])  30.5 us
    all_to_all x1, waiting for transfers between devices, shards(): lax.all_to_all(head_output, 'seq', split_axis=0, concat_axis=1, tiled=True)  23.4 us
    all_gather x1, waiting for transfers between devices, shards(): lax.all_gather(activated[:, inner_width:], 'seq', axis=0, tiled=True)  18.2 us
    reshape x2, local copies, waits for them, and re-layouts, dual_form(): result = (inside + outside).reshape(row_count, head_count, head_width)  7.34 us
    dot_general x1, matrix products, dual_form(): jnp.einsum('chts,cshp->cthp', mixing, block_values, precision=highest)  6.18 us
    all_to_all x1, starting transfers between devices, shards(): lax.all_to_all(step_input, 'seq', split_axis=1, concat_axis=0, tiled=True)  5.95 us
    ppermute x15, waiting for transfers between devices, exchange_in_pairs(): lax.ppermute(sent, axis, [(i, i ^ step) for i in range(length)])  5.74 us
    convert_element_type x1, other arithmetic, convolve(): return jax.nn.silu(mixed).astype(jnp.bfloat16)  5.49 us
  transfers between devices with their start and end apart: 19, of which 5 were waited for; matrix products, arithmetic and copies ran while one was open for 13% of the time, Pallas kernels for 0%

profile of v1, /device:TPU:0, one launch (start us, length us, event | category | flops | bytes accessed | tf_op | source)
XLA Modules:
  0.0 165.9 jit_solution(14819329394867641315)
XLA Ops:
  7.5 4.8 %collective-permute-start = (bf16[3,4352]{1,0:T(4,128)(2,1)S(1)}, bf16[3,4352]{1,0:T(4,128)(2,1)S(1)}, u32[]{:S(2)}, u32[]{:S(2)}) collective-permute-start(bf16[3,4352]{1,0:T(4,128)(2,1)S(1)} %slice.49), channel_id=1, source_target_pairs={{0,2},{2,4},{4,6},{6,8},{8,10},{10,12},{12,14},{14,16},{16,18},{18... | collective-permute-start | bytes 78344 | tf_op jit(solution)/shard_map/ppermute | solution.py:38
  12.3 6.0 %all-to-all-start = ((bf16[128,16,4]{0,2,1:T(4,128)(2,1)}), bf16[128,16,4]{0,2,1:T(4,128)(2,1)S(1)}, u32[]{:S(2)}, u32[]{:S(2)}) async-start(bf16[128,16,4]{0,2,1:T(4,128)(2,1)} %bitcast.135), calls=%async_computation | async-start | bytes 32768 | tf_op jit(solution)/shard_map/all_to_all | solution.py:112
  23.8 5.5 %multiply_convert_fusion = bf16[128,4352]{0,1:T(8,128)(2,1)S(1)} fusion(f32[131,4352]{0,1:T(8,128)S(1)} %maximum_convert_fusion, f32[4352]{0:T(1024)S(1)} %get-tuple-element.7, f32[4352]{0:T(1024)S(1)} %get-tuple-element.8, f32[4352]{0:T(1024)S(1)} %get-tuple-element.6, f32[4352]{0:T(1024)S(1)} %get-tuple-element.5, f32[4352]{0:T(1024)S(1)} %copy-done.4), kind=kLoop, calls=%fused_computation.24 | loop fusion | flops 7241728 | bytes 10114048 | tf_op jit(solution)/shard_map/convert_element_type | solution.py:55
  30.6 2.0 %collective-permute-start.1 = (bf16[128,256]{1,0:T(8,128)(2,1)S(1)}, bf16[128,256]{1,0:T(8,128)(2,1)S(1)}, u32[]{:S(2)}, u32[]{:S(2)}) collective-permute-start(bf16[128,256]{1,0:T(8,128)(2,1)S(1)} %bitcast.133), channel_id=1, source_target_pairs={{0,2},{2,0},{4,6},{6,4},{8,10},{10,8},{12,14},{14,12},{16,18},{18,... | collective-permute-start | bytes 196616 | tf_op jit(solution)/shard_map/ppermute | solution.py:30
  34.6 2.0 %collective-permute-start.4 = (bf16[128,256]{1,0:T(8,128)(2,1)S(1)}, bf16[128,256]{1,0:T(8,128)(2,1)S(1)}, u32[]{:S(2)}, u32[]{:S(2)}) collective-permute-start(bf16[128,256]{1,0:T(8,128)(2,1)S(1)} %bitcast.130), channel_id=1, source_target_pairs={{0,8},{2,10},{4,12},{6,14},{8,0},{10,2},{12,4},{14,6},{16,24},{18,... | collective-permute-start | bytes 196616 | tf_op jit(solution)/shard_map/ppermute | solution.py:30
  39.6 2.3 %reduce-window.6 = f32[8,4,2,128]{3,0,1,2:T(8,128)S(1)} reduce-window(f32[8,4,2,128]{3,0,1,2:T(8,128)S(1)} %copy.84, f32[]{:T(128)} %constant.62.clone.1), window={size=1x1x1x128 pad=0_0x0_0x0_0x127_0}, to_apply=%region_0.1 | reduce-window | flops 1040384 | bytes 65540 | tf_op jit(solution)/shard_map/reduce-window
  42.6 2.4 %collective-permute-start.6 = (bf16[128,256]{1,0:T(8,128)(2,1)S(1)}, bf16[128,256]{1,0:T(8,128)(2,1)S(1)}, u32[]{:S(2)}, u32[]{:S(2)}) collective-permute-start(bf16[128,256]{1,0:T(8,128)(2,1)S(1)} %bitcast.128), channel_id=1, source_target_pairs={{0,12},{2,14},{4,8},{6,10},{8,4},{10,6},{12,0},{14,2},{16,28},{18,... | collective-permute-start | bytes 196616 | tf_op jit(solution)/shard_map/ppermute | solution.py:30
  45.2 2.9 %collective-permute-start.8 = (bf16[128,256]{1,0:T(8,128)(2,1)S(1)}, bf16[128,256]{1,0:T(8,128)(2,1)S(1)}, u32[]{:S(2)}, u32[]{:S(2)}) collective-permute-start(bf16[128,256]{1,0:T(8,128)(2,1)S(1)} %bitcast.126), channel_id=1, source_target_pairs={{0,16},{2,18},{4,20},{6,22},{8,24},{10,26},{12,28},{14,30},{16,0},... | collective-permute-start | bytes 196616 | tf_op jit(solution)/shard_map/ppermute | solution.py:30
  49.7 3.3 %collective-permute-start.10 = (bf16[128,256]{1,0:T(8,128)(2,1)S(1)}, bf16[128,256]{1,0:T(8,128)(2,1)S(1)}, u32[]{:S(2)}, u32[]{:S(2)}) collective-permute-start(bf16[128,256]{1,0:T(8,128)(2,1)S(1)} %bitcast.124), channel_id=1, source_target_pairs={{0,20},{2,22},{4,16},{6,18},{8,28},{10,30},{12,24},{14,26},{16,4},... | collective-permute-start | bytes 196616 | tf_op jit(solution)/shard_map/ppermute | solution.py:30
  53.2 3.8 %collective-permute-start.12 = (bf16[128,256]{1,0:T(8,128)(2,1)S(1)}, bf16[128,256]{1,0:T(8,128)(2,1)S(1)}, u32[]{:S(2)}, u32[]{:S(2)}) collective-permute-start(bf16[128,256]{1,0:T(8,128)(2,1)S(1)} %bitcast.122), channel_id=1, source_target_pairs={{0,24},{2,26},{4,28},{6,30},{8,16},{10,18},{12,20},{14,22},{16,8},... | collective-permute-start | bytes 196616 | tf_op jit(solution)/shard_map/ppermute | solution.py:30
  58.8 5.0 %collective-permute-start.14 = (bf16[128,256]{1,0:T(8,128)(2,1)S(1)}, bf16[128,256]{1,0:T(8,128)(2,1)S(1)}, u32[]{:S(2)}, u32[]{:S(2)}) collective-permute-start(bf16[128,256]{1,0:T(8,128)(2,1)S(1)} %bitcast.120), channel_id=1, source_target_pairs={{0,28},{2,30},{4,24},{6,26},{8,20},{10,22},{12,16},{14,18},{16,12}... | collective-permute-start | bytes 196616 | tf_op jit(solution)/shard_map/ppermute | solution.py:30
  63.8 2.5 %collective-permute-start.15 = (bf16[128,256]{1,0:T(8,128)(2,1)S(1)}, bf16[128,256]{1,0:T(8,128)(2,1)S(1)}, u32[]{:S(2)}, u32[]{:S(2)}) collective-permute-start(bf16[128,256]{1,0:T(8,128)(2,1)S(1)} %bitcast.119), channel_id=1, source_target_pairs={{0,30},{2,28},{4,26},{6,24},{8,22},{10,20},{12,18},{14,16},{16,14}... | collective-permute-start | bytes 196616 | tf_op jit(solution)/shard_map/ppermute | solution.py:30
  67.2 4.6 %collective-permute-done.15 = bf16[128,256]{1,0:T(8,128)(2,1)S(1)} collective-permute-done((bf16[128,256]{1,0:T(8,128)(2,1)S(1)}, bf16[128,256]{1,0:T(8,128)(2,1)S(1)}, u32[]{:S(2)}, u32[]{:S(2)}) %collective-permute-start.15) | collective-permute-done | bytes 65568 | tf_op jit(solution)/shard_map/ppermute | solution.py:30
  76.1 18.2 %all-gather.2.cloned.1.call-done = bf16[2048,256]{0,1:T(8,128)(2,1)} async-done(((bf16[128,256]{0,1:T(8,128)(2,1)}), bf16[2048,256]{0,1:T(8,128)(2,1)}) %all-gather.2.cloned.1.call-update) | async-done | bytes 1048592 | tf_op jit(solution)/shard_map/all_gather | solution.py:114
  94.3 2.3 %fusion.41 = (bf16[2048,128]{0,1:T(8,128)(2,1)}, bf16[2048,128]{0,1:T(8,128)(2,1)}) fusion(bf16[2048,256]{0,1:T(8,128)(2,1)} %all-gather.2.cloned.1.call-done), kind=kLoop, calls=%fused_computation.107 | loop fusion | bytes 2097152 | tf_op jit(solution)/shard_map/slice | solution.py:128
  96.7 2.0 %copy.89 = bf16[2048,128]{1,0:T(8,128)(2,1)} copy(bf16[2048,128]{0,1:T(8,128)(2,1)} %get-tuple-element.25) | data formatting | bytes 1048576 | tf_op jit(solution)/shard_map/slice | solution.py:128
  98.7 2.0 %copy.88 = bf16[2048,128]{1,0:T(8,128)(2,1)} copy(bf16[2048,128]{0,1:T(8,128)(2,1)} %get-tuple-element.26) | data formatting | bytes 1048576 | tf_op jit(solution)/shard_map/slice | solution.py:129
  100.8 2.7 %fusion.20 = f32[8,4,64,128]{3,2,1,0:T(8,128)S(1)} fusion(bf16[8,256,128,1]{2,1,3,0:T(8,128)(2,1)} %bitcast.114, f32[8,256,4,64]{1,0,3,2:T(8,128)S(1)} %convert_multiply_fusion.1), kind=kOutput, calls=%fused_computation.30 | convolution fusion | flops 805306368 | bytes 3670016 | tf_op jit(solution)/shard_map/cshp,csn->chpn/dot_general | solution.py:81
  107.3 6.2 %bitcast_add_fusion = f32[8,256,4,64]{1,3,2,0:T(8,128)S(1)} fusion(f32[8,256,4,64]{1,3,2,0:T(8,128)S(1)} %fusion.24, f32[8,4,256]{2,1,0:T(4,128)S(1)} %copy.90, f32[8,256,256]{2,1,0:T(8,128)S(1)} %fusion.43, f32[8,4,256]{2,1,0:T(4,128)S(1)} %copy.86, pred[256,256]{1,0:T(8,128)(4,1)S(1)} %iota_compare_fusion, bf16[8,256,4,64]{1,0,3,2:T(8,128)(2,1)S(1)} %copy-done.2, ...), kind=kOutput, calls=%fused_computation.29 | convolution fusion | flops 1620049920 | bytes 7503872 | tf_op jit(solution)/shard_map/chts,cshp->cthp/dot_general | solution.py:78
  113.5 3.2 %copy.104 = f32[8,256,4,64]{3,2,1,0:T(4,128)} copy(f32[8,256,4,64]{1,3,2,0:T(8,128)S(1)} %bitcast_add_fusion) | data formatting | bytes 4194304 | tf_op jit(solution)/shard_map/reshape | solution.py:89
  116.7 4.2 %reshape.184 = f32[16,128,256]{2,1,0:T(8,128)S(1)} reshape(f32[8,256,4,64]{3,2,1,0:T(4,128)} %copy.104) | data formatting | bytes 4194304 | tf_op jit(solution)/shard_map/reshape | solution.py:89
  122.1 4.6 %all-to-all-start.1 = ((bf16[16,128,256]{2,1,0:T(8,128)(2,1)}), bf16[16,128,256]{2,1,0:T(8,128)(2,1)S(1)}, u32[]{:S(2)}, u32[]{:S(2)}) async-start(bf16[16,128,256]{2,1,0:T(8,128)(2,1)} %add_convert_fusion), calls=%async_computation.1 | async-start | bytes 2097152 | tf_op jit(solution)/shard_map/all_to_all | solution.py:134
  127.4 23.4 %all-to-all-done.1 = bf16[16,128,256]{2,1,0:T(8,128)(2,1)S(1)} async-done(((bf16[16,128,256]{2,1,0:T(8,128)(2,1)}), bf16[16,128,256]{2,1,0:T(8,128)(2,1)S(1)}, u32[]{:S(2)}, u32[]{:S(2)}) %all-to-all-start.1) | async-done | bytes 1048608 | tf_op jit(solution)/shard_map/all_to_all | solution.py:134
  156.8 2.3 %copy.100 = bf16[128,4096]{1,0:T(8,128)(2,1)} copy(bf16[128,4096]{0,1:T(8,128)(2,1)} %multiply_convert_fusion.1) | data formatting | bytes 2097152 | tf_op jit(solution)/shard_map/convert_element_type | solution.py:44
  (121 shorter events, 33.7 us)
Async XLA Ops:
  6.5 15.5 %copy-start.6 = (f32[64]{0:T(128)S(1)}, f32[64]{0:T(128)}, u32[]{:S(2)}) copy-start(f32[64]{0:T(128)} %param.14) | copy-start | bytes 772
  6.5 15.6 %copy-start.7 = (f32[64]{0:T(128)S(1)}, f32[64]{0:T(128)}, u32[]{:S(2)}) copy-start(f32[64]{0:T(128)} %param.16) | copy-start | bytes 772
  7.5 14.9 %collective-permute-start = (bf16[3,4352]{1,0:T(4,128)(2,1)S(1)}, bf16[3,4352]{1,0:T(4,128)(2,1)S(1)}, u32[]{:S(2)}, u32[]{:S(2)}) collective-permute-start(bf16[3,4352]{1,0:T(4,128)(2,1)S(1)} %slice.49), channel_id=1, source_target_pairs={{0,2},{2,4},{4,6},{6,8},{8,10},{10,12},{12,14},{14,16},{16,18},{18... | collective-permute-start | bytes 78344 | tf_op jit(solution)/shard_map/ppermute | solution.py:38
  12.3 27.1 %all-to-all-start = ((bf16[128,16,4]{0,2,1:T(4,128)(2,1)}), bf16[128,16,4]{0,2,1:T(4,128)(2,1)S(1)}, u32[]{:S(2)}, u32[]{:S(2)}) async-start(bf16[128,16,4]{0,2,1:T(4,128)(2,1)} %bitcast.135), calls=%async_computation | async-start | bytes 32768 | tf_op jit(solution)/shard_map/all_to_all | solution.py:112
  18.3 76.0 %all-gather.2.cloned.1.call-start = ((), (), s32[]{:S(2)}) async-start(), calls=%async_computation.2 | async-start | bytes 1114112 | tf_op jit(solution)/shard_map/all_gather | solution.py:114
  30.6 12.1 %collective-permute-start.1 = (bf16[128,256]{1,0:T(8,128)(2,1)S(1)}, bf16[128,256]{1,0:T(8,128)(2,1)S(1)}, u32[]{:S(2)}, u32[]{:S(2)}) collective-permute-start(bf16[128,256]{1,0:T(8,128)(2,1)S(1)} %bitcast.133), channel_id=1, source_target_pairs={{0,2},{2,0},{4,6},{6,4},{8,10},{10,8},{12,14},{14,12},{16,18},{18,... | collective-permute-start | bytes 196616 | tf_op jit(solution)/shard_map/ppermute | solution.py:30
  32.7 12.4 %collective-permute-start.2 = (bf16[128,256]{1,0:T(8,128)(2,1)S(1)}, bf16[128,256]{1,0:T(8,128)(2,1)S(1)}, u32[]{:S(2)}, u32[]{:S(2)}) collective-permute-start(bf16[128,256]{1,0:T(8,128)(2,1)S(1)} %bitcast.132), channel_id=1, source_target_pairs={{0,4},{2,6},{4,0},{6,2},{8,12},{10,14},{12,8},{14,10},{16,20},{18,... | collective-permute-start | bytes 196616 | tf_op jit(solution)/shard_map/ppermute | solution.py:30
  34.3 10.9 %collective-permute-start.3 = (bf16[128,256]{1,0:T(8,128)(2,1)S(1)}, bf16[128,256]{1,0:T(8,128)(2,1)S(1)}, u32[]{:S(2)}, u32[]{:S(2)}) collective-permute-start(bf16[128,256]{1,0:T(8,128)(2,1)S(1)} %bitcast.131), channel_id=1, source_target_pairs={{0,6},{2,4},{4,2},{6,0},{8,14},{10,12},{12,10},{14,8},{16,22},{18,... | collective-permute-start | bytes 196616 | tf_op jit(solution)/shard_map/ppermute | solution.py:30
  34.6 13.6 %collective-permute-start.4 = (bf16[128,256]{1,0:T(8,128)(2,1)S(1)}, bf16[128,256]{1,0:T(8,128)(2,1)S(1)}, u32[]{:S(2)}, u32[]{:S(2)}) collective-permute-start(bf16[128,256]{1,0:T(8,128)(2,1)S(1)} %bitcast.130), channel_id=1, source_target_pairs={{0,8},{2,10},{4,12},{6,14},{8,0},{10,2},{12,4},{14,6},{16,24},{18,... | collective-permute-start | bytes 196616 | tf_op jit(solution)/shard_map/ppermute | solution.py:30
  36.7 13.0 %collective-permute-start.5 = (bf16[128,256]{1,0:T(8,128)(2,1)S(1)}, bf16[128,256]{1,0:T(8,128)(2,1)S(1)}, u32[]{:S(2)}, u32[]{:S(2)}) collective-permute-start(bf16[128,256]{1,0:T(8,128)(2,1)S(1)} %bitcast.129), channel_id=1, source_target_pairs={{0,10},{2,8},{4,14},{6,12},{8,2},{10,0},{12,6},{14,4},{16,26},{18,... | collective-permute-start | bytes 196616 | tf_op jit(solution)/shard_map/ppermute | solution.py:30
  42.6 10.4 %collective-permute-start.6 = (bf16[128,256]{1,0:T(8,128)(2,1)S(1)}, bf16[128,256]{1,0:T(8,128)(2,1)S(1)}, u32[]{:S(2)}, u32[]{:S(2)}) collective-permute-start(bf16[128,256]{1,0:T(8,128)(2,1)S(1)} %bitcast.128), channel_id=1, source_target_pairs={{0,12},{2,14},{4,8},{6,10},{8,4},{10,6},{12,0},{14,2},{16,28},{18,... | collective-permute-start | bytes 196616 | tf_op jit(solution)/shard_map/ppermute | solution.py:30
  45.1 8.1 %collective-permute-start.7 = (bf16[128,256]{1,0:T(8,128)(2,1)S(1)}, bf16[128,256]{1,0:T(8,128)(2,1)S(1)}, u32[]{:S(2)}, u32[]{:S(2)}) collective-permute-start(bf16[128,256]{1,0:T(8,128)(2,1)S(1)} %bitcast.127), channel_id=1, source_target_pairs={{0,14},{2,12},{4,10},{6,8},{8,6},{10,4},{12,2},{14,0},{16,30},{18,... | collective-permute-start | bytes 196616 | tf_op jit(solution)/shard_map/ppermute | solution.py:30
  45.2 11.8 %collective-permute-start.8 = (bf16[128,256]{1,0:T(8,128)(2,1)S(1)}, bf16[128,256]{1,0:T(8,128)(2,1)S(1)}, u32[]{:S(2)}, u32[]{:S(2)}) collective-permute-start(bf16[128,256]{1,0:T(8,128)(2,1)S(1)} %bitcast.126), channel_id=1, source_target_pairs={{0,16},{2,18},{4,20},{6,22},{8,24},{10,26},{12,28},{14,30},{16,0},... | collective-permute-start | bytes 196616 | tf_op jit(solution)/shard_map/ppermute | solution.py:30
  48.1 10.6 %collective-permute-start.9 = (bf16[128,256]{1,0:T(8,128)(2,1)S(1)}, bf16[128,256]{1,0:T(8,128)(2,1)S(1)}, u32[]{:S(2)}, u32[]{:S(2)}) collective-permute-start(bf16[128,256]{1,0:T(8,128)(2,1)S(1)} %bitcast.125), channel_id=1, source_target_pairs={{0,18},{2,16},{4,22},{6,20},{8,26},{10,24},{12,30},{14,28},{16,2},... | collective-permute-start | bytes 196616 | tf_op jit(solution)/shard_map/ppermute | solution.py:30
  49.7 14.2 %collective-permute-start.10 = (bf16[128,256]{1,0:T(8,128)(2,1)S(1)}, bf16[128,256]{1,0:T(8,128)(2,1)S(1)}, u32[]{:S(2)}, u32[]{:S(2)}) collective-permute-start(bf16[128,256]{1,0:T(8,128)(2,1)S(1)} %bitcast.124), channel_id=1, source_target_pairs={{0,20},{2,22},{4,16},{6,18},{8,28},{10,30},{12,24},{14,26},{16,4},... | collective-permute-start | bytes 196616 | tf_op jit(solution)/shard_map/ppermute | solution.py:30
  53.0 14.0 %collective-permute-start.11 = (bf16[128,256]{1,0:T(8,128)(2,1)S(1)}, bf16[128,256]{1,0:T(8,128)(2,1)S(1)}, u32[]{:S(2)}, u32[]{:S(2)}) collective-permute-start(bf16[128,256]{1,0:T(8,128)(2,1)S(1)} %bitcast.123), channel_id=1, source_target_pairs={{0,22},{2,20},{4,18},{6,16},{8,30},{10,28},{12,26},{14,24},{16,6},... | collective-permute-start | bytes 196616 | tf_op jit(solution)/shard_map/ppermute | solution.py:30
  53.2 13.9 %collective-permute-start.12 = (bf16[128,256]{1,0:T(8,128)(2,1)S(1)}, bf16[128,256]{1,0:T(8,128)(2,1)S(1)}, u32[]{:S(2)}, u32[]{:S(2)}) collective-permute-start(bf16[128,256]{1,0:T(8,128)(2,1)S(1)} %bitcast.122), channel_id=1, source_target_pairs={{0,24},{2,26},{4,28},{6,30},{8,16},{10,18},{12,20},{14,22},{16,8},... | collective-permute-start | bytes 196616 | tf_op jit(solution)/shard_map/ppermute | solution.py:30
  57.0 10.1 %collective-permute-start.13 = (bf16[128,256]{1,0:T(8,128)(2,1)S(1)}, bf16[128,256]{1,0:T(8,128)(2,1)S(1)}, u32[]{:S(2)}, u32[]{:S(2)}) collective-permute-start(bf16[128,256]{1,0:T(8,128)(2,1)S(1)} %bitcast.121), channel_id=1, source_target_pairs={{0,26},{2,24},{4,30},{6,28},{8,18},{10,16},{12,22},{14,20},{16,10}... | collective-permute-start | bytes 196616 | tf_op jit(solution)/shard_map/ppermute | solution.py:30
  58.8 8.4 %collective-permute-start.14 = (bf16[128,256]{1,0:T(8,128)(2,1)S(1)}, bf16[128,256]{1,0:T(8,128)(2,1)S(1)}, u32[]{:S(2)}, u32[]{:S(2)}) collective-permute-start(bf16[128,256]{1,0:T(8,128)(2,1)S(1)} %bitcast.120), channel_id=1, source_target_pairs={{0,28},{2,30},{4,24},{6,26},{8,20},{10,22},{12,16},{14,18},{16,12}... | collective-permute-start | bytes 196616 | tf_op jit(solution)/shard_map/ppermute | solution.py:30
  63.8 8.0 %collective-permute-start.15 = (bf16[128,256]{1,0:T(8,128)(2,1)S(1)}, bf16[128,256]{1,0:T(8,128)(2,1)S(1)}, u32[]{:S(2)}, u32[]{:S(2)}) collective-permute-start(bf16[128,256]{1,0:T(8,128)(2,1)S(1)} %bitcast.119), channel_id=1, source_target_pairs={{0,30},{2,28},{4,26},{6,24},{8,22},{10,20},{12,18},{14,16},{16,14}... | collective-permute-start | bytes 196616 | tf_op jit(solution)/shard_map/ppermute | solution.py:30
  100.8 4.3 %copy-start.1 = (bf16[2048,128]{1,0:T(8,128)(2,1)S(1)}, bf16[2048,128]{1,0:T(8,128)(2,1)}, u32[]{:S(2)}) copy-start(bf16[2048,128]{1,0:T(8,128)(2,1)} %copy.88) | copy-start | bytes 1572868
  106.1 1.2 copy-start.2
  122.1 4.6 %copy-start.3 = (bf16[128,4096]{1,0:T(8,128)(2,1)S(1)}, bf16[128,4096]{1,0:T(8,128)(2,1)}, u32[]{:S(2)}) copy-start(bf16[128,4096]{1,0:T(8,128)(2,1)} %param.10) | copy-start | bytes 3145732
  122.1 28.7 %all-to-all-start.1 = ((bf16[16,128,256]{2,1,0:T(8,128)(2,1)}), bf16[16,128,256]{2,1,0:T(8,128)(2,1)S(1)}, u32[]{:S(2)}, u32[]{:S(2)}) async-start(bf16[16,128,256]{2,1,0:T(8,128)(2,1)} %add_convert_fusion), calls=%async_computation.1 | async-start | bytes 2097152 | tf_op jit(solution)/shard_map/all_to_all | solution.py:134
  (3 other events, 2.6 us)
Sparse Core Ops, SparseCore 0:
  39.5 54.7 all-gather.1
